TPU v7x, 32 devices: a whole 2x2x4 slice. The times are simulated.
32 devices in a mesh: fsdp: 8 (over z, x), tensor: 4 (over y, core).
Axes of the slice: x: 2, y: 2, z: 4, core: 2. Of those that a mesh axis runs over, the one named last changes fastest.
Arguments:
- layer_input: bfloat16 [8192, 1024], P(('fsdp', 'tensor')), may hold values from -6 to 6
- segment_ids: int32 [8, 1024], P('fsdp'), may hold values from 0 to 3, never falling along the last dimension, each value on 1 to 512 neighbouring positions
- pad_mask: int32 [8, 1024], P('fsdp'), may hold values 0 or 1
- attn_gain: float32 [1, 1024], replicated, may hold values from 0.1 to 1.9
- ffn_gain: float32 [1, 1024], replicated, may hold values from 0.1 to 1.9
- out_gain: float32 [1, 128], replicated, may hold values from 0.1 to 1.9
- qkv_weight: bfloat16 [1, 3, 1024, 1024], P(None, None, 'fsdp', 'tensor'), may hold values from -0.1875 to 0.1875
- beta_weight: bfloat16 [1, 1024, 8], P(None, 'fsdp', 'tensor'), may hold values from -0.1875 to 0.1875
- conv_weight: float32 [1, 3, 4, 1024], P(None, None, None, 'tensor'), may hold values from -3 to 3
- out_weight: bfloat16 [1, 1024, 1024], P(None, 'tensor', 'fsdp'), may hold values from -0.1875 to 0.1875
- expand_weight: bfloat16 [1, 2, 1024, 2816], P(None, None, 'fsdp', 'tensor'), may hold values from -0.1875 to 0.1875
- down_weight: bfloat16 [1, 2816, 1024], P(None, 'tensor', 'fsdp'), may hold values from -0.15625 to 0.15625
- cotangent: bfloat16 [8192, 1024], P(('fsdp', 'tensor')), may hold values from -6 to 6
Outputs:
- block_outs: bfloat16 [1, 8192, 1024], P(None, ('fsdp', 'tensor'))
- input_grad: float32 [8192, 1024], P(('fsdp', 'tensor'))
- attn_gain_grad: float32 [1, 1024], replicated
- ffn_gain_grad: float32 [1, 1024], replicated
- out_gain_grad: float32 [1, 128], replicated
- qkv_grad: float32 [1, 3, 1024, 1024], P(None, None, 'fsdp', 'tensor')
- beta_grad: float32 [1, 1024, 8], P(None, 'fsdp', 'tensor')
- conv_grad: float32 [1, 3, 4, 1024], P(None, None, None, 'tensor')
- out_grad: float32 [1, 1024, 1024], P(None, 'tensor', 'fsdp')
- expand_grad: float32 [1, 2, 1024, 2816], P(None, None, 'fsdp', 'tensor')
- down_grad: float32 [1, 2816, 1024], P(None, 'tensor', 'fsdp')
Inputs may be any that keep to these rules, and one draw needn't show every extreme that they name: `segment_ids`: along each sequence the ids never fall; every id from 0 to 3 occurs on 1 to 512 consecutive tokens.
All inputs are finite; a program needn't handle non-finite values. No bound on the sum of `pad_mask` on one device may be relied on, other than what follows from the above.
Results may differ from a plain program's by a relative error of at most 0.012.
Values may be sent and summed in bfloat16 or wider, within the bound.
No kernel may reach another device: no remote copies, remote signals or barrier semaphores. Data moves between devices by JAX's collectives and lax.ppermute only.
A program may use at most 128 MiB of HBM per device.

v0:
```python
import jax
import jax.numpy as jnp
from jax import lax
from jax.sharding import PartitionSpec as P

HEAD = 128
SPAN = 64
highest_precision = lax.Precision.HIGHEST


def rms_norm(value_rows, gain):
    return (
        value_rows
        * lax.rsqrt(jnp.mean(value_rows * value_rows, axis=-1, keepdims=True) + 1e-06)
        * gain
    )


def conv_silu(value_rows, kernel, segments):
    tap_count = kernel.shape[0]
    seq_len = value_rows.shape[1]
    padded = jnp.pad(value_rows, ((0, 0), (tap_count - 1, 0), (0, 0)))
    seg_pad = jnp.concatenate(
        [jnp.full((segments.shape[0], tap_count - 1), -1, jnp.int32), segments], axis=1
    )
    summed = jnp.zeros_like(value_rows)
    for offset in range(tap_count):
        start_at = tap_count - 1 - offset
        same_doc = (seg_pad[:, start_at : start_at + seq_len] == segments).astype(value_rows.dtype)
        summed = (
            summed
            + kernel[offset] * padded[:, start_at : start_at + seq_len] * same_doc[:, :, None]
        )
    return jax.nn.silu(summed)


def unit_rows(value_rows):
    return value_rows * lax.rsqrt(jnp.sum(value_rows * value_rows, axis=-1, keepdims=True) + 1e-06)


def delta_spans(queries, key_vecs, value_vecs, beta_vals, segments):
    members, seq_len, head_dim = key_vecs.shape
    block_count = seq_len // SPAN

    def blocked(value_rows):
        return jnp.moveaxis(
            value_rows.reshape((members, block_count, SPAN) + value_rows.shape[2:]), 1, 0
        )

    identity = jnp.eye(SPAN, dtype=key_vecs.dtype)
    causal = jnp.tril(jnp.ones((SPAN, SPAN), key_vecs.dtype))

    def advance(carried, block):
        memory_state, previous = carried
        query_block, key_block, value_blk, beta_blk, seg_blk = block
        same_doc = (seg_blk[:, :, None] == seg_blk[:, None, :]).astype(key_block.dtype)
        leading_shape = (seg_blk == previous[:, None]).astype(key_block.dtype)
        trailing_shape = (seg_blk == seg_blk[:, -1:]).astype(key_block.dtype)
        products = jnp.einsum("nid,njd->nij", key_block, key_block, precision=highest_precision)
        system = identity + jnp.tril(beta_blk[:, :, None] * products * same_doc, -1)
        recalled_values = jnp.einsum(
            "vhr,vcr->vch", memory_state, key_block, precision=highest_precision
        )
        right_side = beta_blk[:, :, None] * (
            value_blk - leading_shape[:, :, None] * recalled_values
        )
        state_update = jax.scipy.linalg.solve_triangular(
            system, right_side, lower=True, unit_diagonal=True
        )
        score_matrix = (
            jnp.einsum("nid,njd->nij", query_block, key_block, precision=highest_precision)
            * same_doc
            * causal
        )
        output_rows = leading_shape[:, :, None] * jnp.einsum(
            "vhr,vcr->vch", memory_state, query_block, precision=highest_precision
        ) + jnp.einsum("fwu,fug->fwg", score_matrix, state_update, precision=highest_precision)
        memory_state = leading_shape[:, -1][:, None, None] * memory_state + jnp.einsum(
            "ytz,ytv->yzv",
            state_update * trailing_shape[:, :, None],
            key_block,
            precision=highest_precision,
        )
        return ((memory_state, seg_blk[:, -1]), output_rows)

    start_mem = jnp.zeros((members, head_dim, head_dim), key_vecs.dtype)
    start_seg = jnp.full((members,), -1, jnp.int32)
    carried, outputs = lax.scan(
        jax.checkpoint(advance),
        (start_mem, start_seg),
        (
            blocked(queries),
            blocked(key_vecs),
            blocked(value_vecs),
            blocked(beta_vals),
            blocked(segments),
        ),
    )
    return jnp.moveaxis(outputs, 0, 1).reshape(members, seq_len, head_dim)


def mixer(query_pre, key_pre, value_pre, logits, kernels, gain_out, segments, pad_mask):
    batch_size, seq_len, channels = query_pre.shape
    head_count = channels // HEAD

    def heads_first(value_rows):
        return (
            value_rows.reshape(batch_size, seq_len, head_count, HEAD)
            .transpose(0, 2, 1, 3)
            .reshape(batch_size * head_count, seq_len, HEAD)
        )

    queries = unit_rows(heads_first(conv_silu(query_pre, kernels[0], segments)))
    key_vecs = unit_rows(heads_first(conv_silu(key_pre, kernels[1], segments)))
    value_vecs = heads_first(conv_silu(value_pre, kernels[2], segments))
    beta_vals = (
        (jax.nn.sigmoid(logits) * pad_mask.astype(logits.dtype)[:, :, None])
        .transpose(0, 2, 1)
        .reshape(batch_size * head_count, seq_len)
    )
    seg_rep = jnp.repeat(segments, head_count, axis=0)
    output_rows = delta_spans(queries, key_vecs, value_vecs, beta_vals, seg_rep)
    output_rows = (
        output_rows
        * lax.rsqrt(jnp.mean(output_rows * output_rows, axis=-1, keepdims=True) + 1e-05)
        * gain_out
    )
    return (
        output_rows.reshape(batch_size, head_count, seq_len, HEAD)
        .transpose(0, 2, 1, 3)
        .reshape(batch_size, seq_len, channels)
    )


def spread_rows(normed):
    return lax.all_gather(normed, "tensor", axis=0, tiled=True)


def collect_rows(term_fn, row_count):
    return lax.psum_scatter(
        term_fn(jnp.int32(0), lax.axis_size("tensor") * row_count),
        "tensor",
        scatter_dimension=0,
        tiled=True,
    )


def spread_grad(gradient):
    return lax.all_gather(gradient, "tensor", axis=0, tiled=True)


def collect_grad(term_fn, row_count):
    return lax.psum_scatter(
        term_fn(jnp.int32(0), lax.axis_size("tensor") * row_count),
        "tensor",
        scatter_dimension=0,
        tiled=True,
    )


def on_device(
    layer_input,
    segment_ids,
    pad_mask,
    attn_gain,
    ffn_gain,
    out_gain,
    qkv_weight,
    beta_weight,
    conv_weight,
    out_weight,
    expand_weight,
    down_weight,
    cotangent,
):
    layer_count = qkv_weight.shape[0]
    row_count = layer_input.shape[0]
    resid = layer_input.astype(jnp.float32)
    layer_index = 0
    matrices = (
        lax.all_gather(qkv_weight[layer_index], "fsdp", axis=1, tiled=True),
        lax.all_gather(beta_weight[layer_index], "fsdp", axis=0, tiled=True),
        lax.all_gather(expand_weight[layer_index], "fsdp", axis=1, tiled=True),
        lax.all_gather(out_weight[layer_index], "fsdp", axis=1, tiled=True),
        lax.all_gather(down_weight[layer_index], "fsdp", axis=1, tiled=True),
    )
    qkv_full, beta_full, expand_full, out_full, down_full = matrices
    normed = rms_norm(resid, attn_gain[layer_index]).astype(jnp.bfloat16)
    gathered = spread_rows(normed)
    projected = jnp.einsum("ld,sdc->slc", gathered, qkv_full, preferred_element_type=jnp.float32)
    logits = jnp.dot(gathered, beta_full, preferred_element_type=jnp.float32)

    def local_mix(query_pre, key_pre, value_pre, logit_vals, kernels, gain_out):
        return mixer(
            query_pre[None],
            key_pre[None],
            value_pre[None],
            logit_vals[None],
            kernels,
            gain_out,
            segment_ids,
            pad_mask,
        )[0]

    mixed_tokens, pullback = jax.vjp(
        local_mix,
        projected[0],
        projected[1],
        projected[2],
        logits,
        conv_weight[layer_index],
        out_gain[layer_index],
    )
    mixed_low = mixed_tokens.astype(jnp.bfloat16)

    def attn_term(start, count):
        return jnp.dot(mixed_low, out_full, preferred_element_type=jnp.float32)

    resid_mid = resid + collect_rows(attn_term, row_count)
    token_mixed = mixed_low
    out_entire = out_full
    normed_ffn = rms_norm(resid_mid, ffn_gain[layer_index]).astype(jnp.bfloat16)
    gathered_ffn = spread_rows(normed_ffn)
    expanded = jnp.einsum(
        "ld,sdf->slf", gathered_ffn, expand_full, preferred_element_type=jnp.float32
    )
    hidden = (jax.nn.silu(expanded[0]) * expanded[1]).astype(jnp.bfloat16)

    def ffn_term(start, count):
        return jnp.dot(hidden, down_full, preferred_element_type=jnp.float32)

    resid_out = resid_mid + collect_rows(ffn_term, row_count)
    stored = [
        (
            resid,
            gathered,
            pullback,
            mixed_low,
            resid_mid,
            gathered_ffn,
            expanded,
            hidden,
            matrices,
            token_mixed,
            out_entire,
        )
    ]
    block_outs = [resid_out.astype(jnp.bfloat16)]
    gradient = cotangent.astype(jnp.float32)
    weight_parts = [None] * layer_count
    conv_parts = [None] * layer_count
    attn_parts = [None] * layer_count
    ffn_parts = [None] * layer_count
    head_parts = [None] * layer_count
    layer_index = 0
    (
        resid,
        gathered,
        pullback,
        mixed_low,
        resid_mid,
        gathered_ffn,
        expanded,
        hidden,
        matrices,
        token_mixed,
        out_entire,
    ) = stored[layer_index]
    matrices = (
        lax.all_gather(qkv_weight[layer_index], "fsdp", axis=1, tiled=True),
        lax.all_gather(beta_weight[layer_index], "fsdp", axis=0, tiled=True),
        lax.all_gather(expand_weight[layer_index], "fsdp", axis=1, tiled=True),
        lax.all_gather(out_weight[layer_index], "fsdp", axis=1, tiled=True),
        lax.all_gather(down_weight[layer_index], "fsdp", axis=1, tiled=True),
    )
    qkv_full, beta_full, expand_full, out_full, down_full = matrices
    grad_full = spread_grad(gradient.astype(jnp.bfloat16))
    d_hidden = lax.dot_general(
        grad_full, down_full, (((1,), (1,)), ((), ())), preferred_element_type=jnp.float32
    )
    d_down = lax.dot_general(
        hidden, grad_full, (((0,), (0,)), ((), ())), preferred_element_type=jnp.float32
    )
    gate_vals = expanded[0]
    up_vals = expanded[1]
    sig_gate = jax.nn.sigmoid(gate_vals)
    d_gate = d_hidden * up_vals * sig_gate * (1.0 + gate_vals * (1.0 - sig_gate))
    d_up = d_hidden * gate_vals * sig_gate
    d_expanded = jnp.stack([d_gate, d_up]).astype(jnp.bfloat16)
    d_expand = jnp.einsum(
        "ld,slf->sdf", gathered_ffn, d_expanded, preferred_element_type=jnp.float32
    )

    def ffn_back(start, count):
        return jnp.einsum(
            "slf,sdf->ld", d_expanded, expand_full, preferred_element_type=jnp.float32
        )

    d_normed_ffn = collect_grad(ffn_back, row_count)
    unused, norm_back = jax.vjp(rms_norm, resid_mid, ffn_gain[layer_index])
    d_resid_mid, d_ffn_gain = norm_back(d_normed_ffn)
    gradient = gradient + d_resid_mid
    grad_low = gradient.astype(jnp.bfloat16)
    grad_full = spread_grad(grad_low)
    d_mixed = lax.dot_general(
        grad_full, out_full, (((1,), (1,)), ((), ())), preferred_element_type=jnp.float32
    )
    d_out = lax.dot_general(
        mixed_low, grad_full, (((0,), (0,)), ((), ())), preferred_element_type=jnp.float32
    )
    d_query, d_key, d_value, d_logits, d_kernels, d_head_gain = pullback(d_mixed)
    d_projected = jnp.stack([d_query, d_key, d_value]).astype(jnp.bfloat16)
    d_logit_low = d_logits.astype(jnp.bfloat16)
    d_qkv = jnp.einsum("ld,slc->sdc", gathered, d_projected, preferred_element_type=jnp.float32)
    d_beta = lax.dot_general(
        gathered, d_logit_low, (((0,), (0,)), ((), ())), preferred_element_type=jnp.float32
    )

    def attn_back(start, count):
        part_qkv = jnp.einsum(
            "slc,sdc->ld", d_projected, qkv_full, preferred_element_type=jnp.float32
        )
        part_beta = lax.dot_general(
            d_logit_low, beta_full, (((1,), (1,)), ((), ())), preferred_element_type=jnp.float32
        )
        return part_qkv + part_beta

    d_normed = collect_grad(attn_back, row_count)
    unused, norm_back = jax.vjp(rms_norm, resid, attn_gain[layer_index])
    d_resid, d_attn_gain = norm_back(d_normed)
    gradient = gradient + d_resid
    weight_parts[layer_index] = (
        lax.psum_scatter(d_qkv, "fsdp", scatter_dimension=1, tiled=True),
        lax.psum_scatter(d_beta, "fsdp", scatter_dimension=0, tiled=True),
        lax.psum_scatter(d_expand, "fsdp", scatter_dimension=1, tiled=True),
        lax.psum_scatter(d_out, "fsdp", scatter_dimension=1, tiled=True),
        lax.psum_scatter(d_down, "fsdp", scatter_dimension=1, tiled=True),
    )
    conv_parts[layer_index] = d_kernels
    attn_parts[layer_index] = d_attn_gain
    ffn_parts[layer_index] = d_ffn_gain
    head_parts[layer_index] = d_head_gain
    conv_total = lax.psum(jnp.stack(conv_parts), "fsdp")
    attn_total, ffn_total, head_total = lax.psum(
        (jnp.stack(attn_parts), jnp.stack(ffn_parts), jnp.stack(head_parts)), ("fsdp", "tensor")
    )
    qkv_total = jnp.stack([parts[0] for parts in weight_parts])
    beta_total = jnp.stack([parts[1] for parts in weight_parts])
    expand_total = jnp.stack([parts[2] for parts in weight_parts])
    out_total = jnp.stack([parts[3] for parts in weight_parts])
    down_total = jnp.stack([parts[4] for parts in weight_parts])
    return (
        jnp.stack(block_outs),
        gradient,
        attn_total,
        ffn_total,
        head_total,
        qkv_total,
        beta_total,
        conv_total,
        out_total,
        expand_total,
        down_total,
    )


def solution(mesh):
    in_specs = (
        P(("fsdp", "tensor"), None),
        P("fsdp", None),
        P("fsdp", None),
        P(),
        P(),
        P(),
        P(None, None, "fsdp", "tensor"),
        P(None, "fsdp", "tensor"),
        P(None, None, None, "tensor"),
        P(None, "tensor", "fsdp"),
        P(None, None, "fsdp", "tensor"),
        P(None, "tensor", "fsdp"),
        P(("fsdp", "tensor"), None),
    )
    out_specs = (
        P(None, ("fsdp", "tensor"), None),
        P(("fsdp", "tensor"), None),
        P(),
        P(),
        P(),
        P(None, None, "fsdp", "tensor"),
        P(None, "fsdp", "tensor"),
        P(None, None, None, "tensor"),
        P(None, "tensor", "fsdp"),
        P(None, None, "fsdp", "tensor"),
        P(None, "tensor", "fsdp"),
    )
    return jax.shard_map(
        on_device, mesh=mesh, in_specs=in_specs, out_specs=out_specs, check_vma=False
    )
```

profile of v0, /device:TPU:0, one launch (start us, length us, event | category | flops | bytes accessed | tf_op | source)
XLA Modules:
  0.0 1515.9 jit_solution(4596001099387857349)
XLA Ops:
  12.7 22.1 %all-gather = bf16[1,1024,2]{1,2,0:T(2,128)(2,1)S(1)} all-gather(bf16[1,128,2]{1,2,0:T(2,128)(2,1)S(1)} %copy-done.35), channel_id=2, replica_groups=mesh['fsdp'=8,'tensor'=4] {'fsdp'}, dimensions={1}, use_global_device_ids=true | all-gather | bytes 4608 | tf_op jit(solution)/shard_map/all_gather | solution.py:182
  35.0 29.6 %all-gather.2 = bf16[1,256,1024]{2,1,0:T(8,128)(2,1)S(1)} all-gather(bf16[1,256,128]{2,1,0:T(8,128)(2,1)S(1)} %copy-done.29), channel_id=4, replica_groups=mesh['fsdp'=8,'tensor'=4] {'fsdp'}, dimensions={2}, use_global_device_ids=true | all-gather | bytes 589824 | tf_op jit(solution)/shard_map/all_gather | solution.py:184
  64.7 22.7 %all-gather.13.cloned.1.call-done = bf16[1024,1024]{1,0:T(8,128)(2,1)} async-done(((bf16[256,1024]{1,0:T(8,128)(2,1)}), bf16[1024,1024]{1,0:T(8,128)(2,1)}) %all-gather.13.cloned.1.call-update) | async-done | bytes 2097168 | tf_op jit(solution)/shard_map/all_gather | solution.py:136
  104.5 255.6 %while.43 = (s32[]{:T(128)}, f32[2,128,128]{2,1,0:T(8,128)S(1)}, s32[2]{0:T(128)S(1)}, f32[16,2,64,128]{3,2,0,1:T(8,128)S(1)}, f32[16,2,128,128]{3,2,1,0:T(8,128...) while((s32[]{:T(128)}, f32[2,128,128]{2,1,0:T(8,128)S(1)}, ...), condition=%wide.region_4.6_spmd.clone, body=%wide.region_3.5_spmd.clone.sunk | while | flops 126235200 | bytes 2117866 | solution.py:88
  104.9 9.8 custom-call.26
  120.9 9.8 custom-call.26
  136.9 9.8 custom-call.26
  152.9 9.8 custom-call.26
  168.9 9.8 custom-call.26
  184.8 9.8 custom-call.26
  200.8 9.8 custom-call.26
  216.8 9.8 custom-call.26
  232.8 9.8 custom-call.26
  248.7 9.8 custom-call.26
  264.7 9.8 custom-call.26
  280.7 9.8 custom-call.26
  296.7 9.8 custom-call.26
  312.6 9.8 custom-call.26
  328.6 9.8 custom-call.26
  344.6 9.8 custom-call.26
  366.5 44.0 %reduce-scatter.12.cloned.1.call-done = f32[256,1024]{1,0:T(8,128)} async-done(((f32[1024,1024]{1,0:T(8,128)}), f32[256,1024]{1,0:T(8,128)}) %reduce-scatter.12.cloned.1.call-update) | async-done | bytes 1048592 | tf_op jit(solution)/shard_map/reduce_scatter | solution.py:140
  414.6 58.0 %all-gather.23.cloned.1.call-done = bf16[1,2,1024,704]{2,3,1,0:T(8,128)(2,1)} async-done(((bf16[1,2,128,704]{2,3,1,0:T(8,128)(2,1)}), bf16[1,2,1024,704]{2,3,1,0:T(8,128)(2,1)}) %all-gather.23.cloned.1.call-update) | async-done | bytes 2883600 | tf_op jit(solution)/shard_map/all_gather | solution.py:183
  472.6 22.9 %all-gather.15.cloned.1.call-done = bf16[1024,1024]{1,0:T(8,128)(2,1)} async-done(((bf16[256,1024]{1,0:T(8,128)(2,1)}), bf16[1024,1024]{1,0:T(8,128)(2,1)}) %all-gather.15.cloned.1.call-update) | async-done | bytes 2097168 | tf_op jit(solution)/shard_map/all_gather | solution.py:136
  503.6 37.9 %all-gather.25.cloned.1.call-done = bf16[1,704,1024]{2,1,0:T(8,128)(2,1)} async-done(((bf16[1,704,128]{2,1,0:T(8,128)(2,1)}), bf16[1,704,1024]{2,1,0:T(8,128)(2,1)}) %all-gather.25.cloned.1.call-update) | async-done | bytes 1441808 | tf_op jit(solution)/shard_map/all_gather | solution.py:185
  541.4 22.6 %all-gather.17.cloned.1.call-done = bf16[1024,1024]{1,0:T(8,128)(2,1)} async-done(((bf16[256,1024]{1,0:T(8,128)(2,1)}), bf16[1024,1024]{1,0:T(8,128)(2,1)}) %all-gather.17.cloned.1.call-update) | async-done | bytes 2097168 | tf_op jit(solution)/shard_map/all_gather | solution.py:149
  578.5 44.6 %reduce-scatter.16.cloned.1.call-done = f32[256,1024]{1,0:T(8,128)} async-done(((f32[1024,1024]{1,0:T(8,128)}), f32[256,1024]{1,0:T(8,128)}) %reduce-scatter.16.cloned.1.call-update) | async-done | bytes 1048592 | tf_op jit(solution)/shard_map/reduce_scatter | solution.py:153
  626.4 22.2 %all-gather.19.cloned.1.call-done = bf16[1024,1024]{1,0:T(8,128)(2,1)} async-done(((bf16[256,1024]{1,0:T(8,128)(2,1)}), bf16[1024,1024]{1,0:T(8,128)(2,1)}) %all-gather.19.cloned.1.call-update) | async-done | bytes 2097168 | tf_op jit(solution)/shard_map/all_gather | solution.py:149
  658.6 350.7 %while.44 = (s32[]{:T(128)}, f32[2,128,128]{2,1,0:T(8,128)S(1)}, f32[16,2,64,128]{3,2,0,1:T(8,128)}, f32[16,2,64,128]{3,2,0,1:T(8,128)}, f32[16,2,64,128]{3,2,0,...) while((s32[]{:T(128)}, f32[2,128,128]{2,1,0:T(8,128)S(1)}, ...), condition=%wide.region_15.17_spmd.clone, body=%wide.region_12.16_spmd.clone.sunk | while | flops 321565120 | bytes 5879079 | solution.py:88
  663.3 9.8 custom-call.27
  685.2 9.8 custom-call.27
  707.1 9.8 custom-call.27
  729.0 9.8 custom-call.27
  750.9 9.8 custom-call.27
  772.9 9.8 custom-call.27
  794.8 9.8 custom-call.27
  816.7 9.8 custom-call.27
  838.6 9.8 custom-call.27
  860.5 9.8 custom-call.27
  882.5 9.8 custom-call.27
  948.2 9.8 custom-call.27
  992.1 9.8 custom-call.27
  1061.8 37.6 %psum.31 = f32[1,3,4,256]{3,2,1,0:T(4,128)} all-reduce(f32[1,3,4,256]{3,2,1,0:T(4,128)S(1)} %add_bitcast_fusion), channel_id=1, replica_groups=mesh['fsdp'=8,'tensor'=4] {'fsdp'}, use_global_device_ids=true, to_apply=%region_40.42 | all-reduce | flops 3072 | bytes 24576 | tf_op jit(solution)/shard_map/psum | solution.py:343
  1101.5 54.9 %reduce-scatter.20.cloned.1.call-done = f32[3,128,256]{1,2,0:T(8,128)} async-done(((f32[3,1024,256]{1,2,0:T(8,128)}), f32[3,128,256]{1,2,0:T(8,128)}) %reduce-scatter.20.cloned.1.call-update) | async-done | bytes 393232 | tf_op jit(solution)/shard_map/reduce_scatter | solution.py:333
  1158.3 44.3 %reduce-scatter.18.cloned.1.call-done = f32[256,1024]{1,0:T(8,128)} async-done(((f32[1024,1024]{1,0:T(8,128)}), f32[256,1024]{1,0:T(8,128)}) %reduce-scatter.18.cloned.1.call-update) | async-done | bytes 1048592 | tf_op jit(solution)/shard_map/reduce_scatter | solution.py:153
  1204.3 39.8 %all-reduce.31 = (f32[1,1024]{1,0:T(1,128)}, f32[1,1024]{1,0:T(1,128)}, f32[1,128]{1,0:T(1,128)}) all-reduce(f32[1,1024]{1,0:T(1,128)S(1)} %bitcast.553, f32[1,1024]{1,0:T(1,128)S(1)} %bitcast.552, f32[1,128]{1,0:T(1,128)S(1)} %bitcast.593), channel_id=1, replica_groups=mesh['fsdp'=8,'tensor'=4] {'fsdp','tensor'}, use_global_device_ids=true, to_apply=%region_21.23 | all-reduce | flops 2176 | bytes 17408 | tf_op jit(solution)/shard_map/psum | solution.py:344
  1253.5 73.6 %reduce-scatter.26.cloned.1.call-done = f32[704,128]{1,0:T(8,128)} async-done(((f32[704,1024]{1,0:T(8,128)}), f32[704,128]{1,0:T(8,128)}) %reduce-scatter.26.cloned.1.call-update) | async-done | bytes 360464 | tf_op jit(solution)/shard_map/reduce_scatter | solution.py:337
  1327.1 114.0 %reduce-scatter.24.cloned.1.call-done = f32[2,128,704]{1,2,0:T(8,128)} async-done(((f32[2,1024,704]{1,2,0:T(8,128)}), f32[2,128,704]{1,2,0:T(8,128)}) %reduce-scatter.24.cloned.1.call-update) | async-done | bytes 720912 | tf_op jit(solution)/shard_map/reduce_scatter | solution.py:335
  1441.1 68.0 %reduce-scatter.22.cloned.1.call-done = f32[256,128]{1,0:T(8,128)} async-done(((f32[256,1024]{1,0:T(8,128)}), f32[256,128]{1,0:T(8,128)}) %reduce-scatter.22.cloned.1.call-update) | async-done | bytes 131088 | tf_op jit(solution)/shard_map/reduce_scatter | solution.py:336
  (1097 shorter events, 452.4 us)
Async XLA Ops:
  7.2 4.2 copy-start.34
  7.2 4.7 copy-start.31
  7.2 5.5 copy-start.35
  7.2 27.8 %copy-start.32 = (f32[1,3,4,256]{3,2,1,0:T(4,128)S(1)}, f32[1,3,4,256]{3,2,1,0:T(4,128)}, u32[]{:S(2)}) copy-start(f32[1,3,4,256]{3,2,1,0:T(4,128)} %param.27) | copy-start | bytes 36868
  7.2 27.8 %copy-start.29 = (bf16[1,256,128]{2,1,0:T(8,128)(2,1)S(1)}, bf16[1,256,128]{2,1,0:T(8,128)(2,1)}, u32[]{:S(2)}) copy-start(bf16[1,256,128]{2,1,0:T(8,128)(2,1)} %param.28) | copy-start | bytes 196612
  7.2 57.4 %all-gather.21.cloned.1.call-start = ((), (), s32[]{:S(2)}) async-start(), calls=%async_computation.21 | async-start | bytes 1769472 | tf_op jit(solution)/shard_map/all_gather | solution.py:181
  8.0 79.4 %all-gather.13.cloned.1.call-start = ((), (), s32[]{:S(2)}) async-start(), calls=%async_computation.9 | async-start | bytes 2621440 | tf_op jit(solution)/shard_map/all_gather | solution.py:136
  11.3 399.2 %reduce-scatter.12.cloned.1.call-start = ((), (), s32[]{:S(2)}) async-start(), calls=%async_computation.10 | async-start | bytes 5242880 | tf_op jit(solution)/shard_map/reduce_scatter | solution.py:140
  64.7 298.3 %copy-start.21 = (bf16[1,256,1024]{2,1,0:T(8,128)(2,1)}, bf16[1,256,1024]{2,1,0:T(8,128)(2,1)S(1)}, u32[]{:S(2)}) copy-start(bf16[1,256,1024]{2,1,0:T(8,128)(2,1)S(1)} %all-gather.2) | copy-start | bytes 1572868
  91.2 1.7 copy-start.7
  92.9 2.9 copy-start.11
  92.9 2.9 copy-start.13
  92.9 4.8 copy-start.9
  101.6 2.0 copy-start.17
  104.5 256.1 %copy-start.33 = (f32[1,128]{1,0:T(1,128)S(1)}, f32[1,128]{1,0:T(1,128)}, u32[]{:S(2)}) copy-start(f32[1,128]{1,0:T(1,128)} %param.24) | copy-start | bytes 1540
  360.1 5.7 copy-start.20
  363.0 2.8 copy-start.19
  365.8 44.7 %copy-start.5 = (bf16[256,1024]{1,0:T(8,128)(2,1)S(1)}, bf16[256,1024]{1,0:T(8,128)(2,1)}, u32[]{:S(2)}) copy-start(bf16[256,1024]{1,0:T(8,128)(2,1)} %param.19) | copy-start | bytes 1572868
  365.8 46.1 %copy-start.28 = (f32[1,1024]{1,0:T(1,128)S(1)}, f32[1,1024]{1,0:T(1,128)}, u32[]{:S(2)}) copy-start(f32[1,1024]{1,0:T(1,128)} %param.23) | copy-start | bytes 12292
  365.8 106.8 %all-gather.23.cloned.1.call-start = ((), (), s32[]{:S(2)}) async-start(), calls=%async_computation.22 | async-start | bytes 3244032 | tf_op jit(solution)/shard_map/all_gather | solution.py:183
  366.4 129.1 %all-gather.15.cloned.1.call-start = ((), (), s32[]{:S(2)}) async-start(), calls=%async_computation.11 | async-start | bytes 2621440 | tf_op jit(solution)/shard_map/all_gather | solution.py:136
  412.9 128.5 %all-gather.25.cloned.1.call-start = ((), (), s32[]{:S(2)}) async-start(), calls=%async_computation.23 | async-start | bytes 1622016 | tf_op jit(solution)/shard_map/all_gather | solution.py:185
  413.5 150.6 %all-gather.17.cloned.1.call-start = ((), (), s32[]{:S(2)}) async-start(), calls=%async_computation.13 | async-start | bytes 2621440 | tf_op jit(solution)/shard_map/all_gather | solution.py:149
  414.2 208.8 %reduce-scatter.16.cloned.1.call-start = ((), (), s32[]{:S(2)}) async-start(), calls=%async_computation.14 | async-start | bytes 5242880 | tf_op jit(solution)/shard_map/reduce_scatter | solution.py:153
  564.1 9.3 copy-start.36
  578.4 46.2 %copy-start.23 = (bf16[256,1024]{1,0:T(8,128)(2,1)S(1)}, bf16[256,1024]{1,0:T(8,128)(2,1)}, u32[]{:S(2)}) copy-start(bf16[256,1024]{1,0:T(8,128)(2,1)} %param.31) | copy-start | bytes 1572868
  578.4 70.1 %all-gather.19.cloned.1.call-start = ((), (), s32[]{:S(2)}) async-start(), calls=%async_computation.15 | async-start | bytes 2621440 | tf_op jit(solution)/shard_map/all_gather | solution.py:149
  623.0 1.6 copy-start.15
  624.6 23.9 %copy-start.22 = (bf16[1,256,1024]{2,1,0:T(8,128)(2,1)S(1)}, bf16[1,256,1024]{2,1,0:T(8,128)(2,1)}, u32[]{:S(2)}) copy-start(bf16[1,256,1024]{2,1,0:T(8,128)(2,1)} %copy-done.21) | copy-start | bytes 1572868
  625.8 474.0 %reduce-scatter.28.cloned.1.call-start = ((), (), s32[]{:S(2)}) async-start(), calls=%async_computation.24 | async-start | bytes 589824
  653.4 1.9 copy-start
  1009.3 2.1 copy-start.3
  1016.4 140.0 %reduce-scatter.20.cloned.1.call-start = ((), (), s32[]{:S(2)}) async-start(), calls=%async_computation.17 | async-start | bytes 3538944 | tf_op jit(solution)/shard_map/reduce_scatter | solution.py:333
  1016.6 4.2 copy-start.8
  1016.6 4.2 copy-start.10
  1016.6 4.2 copy-start.12
  1016.7 4.2 copy-start.14
  1027.8 1.8 copy-start.18
  1033.1 169.4 %reduce-scatter.18.cloned.1.call-start = ((), (), s32[]{:S(2)}) async-start(), calls=%async_computation.16 | async-start | bytes 5242880 | tf_op jit(solution)/shard_map/reduce_scatter | solution.py:153
  1038.7 211.6 %reduce-scatter.14.cloned.1.call-start = ((), (), s32[]{:S(2)}) async-start(), calls=%async_computation.12 | async-start | bytes 5242880 | tf_op jit(solution)/shard_map/reduce_scatter | solution.py:140
  1044.4 282.7 %reduce-scatter.26.cloned.1.call-start = ((), (), s32[]{:S(2)}) async-start(), calls=%async_computation.20 | async-start | bytes 3244032 | tf_op jit(solution)/shard_map/reduce_scatter | solution.py:337
  1049.7 391.4 %reduce-scatter.24.cloned.1.call-start = ((), (), s32[]{:S(2)}) async-start(), calls=%async_computation.19 | async-start | bytes 6488064 | tf_op jit(solution)/shard_map/reduce_scatter | solution.py:335
  1058.1 41.4 %copy-start.1 = (f32[1,1024,2,128]{3,1,2,0:T(8,128)S(1)}, f32[1,1024,2,128]{3,1,2,0:T(8,128)}, u32[]{:S(2)}) copy-start(f32[1,1024,2,128]{3,1,2,0:T(8,128)} %copy-done) | copy-start | bytes 3145732
  1058.1 451.1 %reduce-scatter.22.cloned.1.call-start = ((), (), s32[]{:S(2)}) async-start(), calls=%async_computation.18 | async-start | bytes 1179648 | tf_op jit(solution)/shard_map/reduce_scatter | solution.py:336
  1061.7 140.8 %copy-start.30 = (f32[1,1024]{1,0:T(1,128)S(1)}, f32[1,1024]{1,0:T(1,128)}, u32[]{:S(2)}) copy-start(f32[1,1024]{1,0:T(1,128)} %param.22) | copy-start | bytes 12292
  1099.8 150.5 %copy-start.6 = (bf16[256,1024]{1,0:T(8,128)(2,1)S(1)}, bf16[256,1024]{1,0:T(8,128)(2,1)}, u32[]{:S(2)}) copy-start(bf16[256,1024]{1,0:T(8,128)(2,1)} %param.19) | copy-start | bytes 1572868
  1099.8 150.5 %copy-start.16 = (f32[256,1024]{1,0:T(8,128)S(1)}, f32[256,1024]{1,0:T(8,128)}, u32[]{:S(2)}) copy-start(f32[256,1024]{1,0:T(8,128)} %reduce-scatter.16.cloned.1.call-done) | copy-start | bytes 3145732
  1099.8 150.5 %copy-start.24 = (bf16[256,1024]{1,0:T(8,128)(2,1)S(1)}, bf16[256,1024]{1,0:T(8,128)(2,1)}, u32[]{:S(2)}) copy-start(bf16[256,1024]{1,0:T(8,128)(2,1)} %param.31) | copy-start | bytes 1572868
  (8 other events, 10.1 us)
Sparse Core Ops, SparseCore 0:
  10.2 50.5 all-gather.20
  62.9 24.3 all-gather.12
  365.9 44.4 reduce-scatter.11
  412.6 60.0 all-gather.22
  474.7 20.7 all-gather.14
  497.6 43.8 all-gather.24
  543.1 20.9 all-gather.16
  578.5 44.4 reduce-scatter.15
  625.9 22.5 all-gather.18
  1016.5 61.9 reduce-scatter.27
  1082.5 73.8 reduce-scatter.19
  1158.9 43.6 reduce-scatter.17
  1205.1 45.1 reduce-scatter.13
  1254.7 72.3 reduce-scatter.25
  1331.6 109.4 reduce-scatter.23
  1445.3 63.7 reduce-scatter.21
where the time goes:
time: 1530 us; the launch traced here: 1520 us
  waiting for transfers between devices  639 us (42%)
  other arithmetic  374 us (24%)
  matrix products  263 us (17%)
  blocking collectives  129 us (8%)
  local copies, waits for them, and re-layouts  89.5 us (6%)
    another operation x112, other arithmetic, advance(): jax.scipy.linalg.solve_triangular(system, right_side, lower=True, unit_di...  319 us
    reduce_scatter x1, waiting for transfers between devices, on_device(): lax.psum_scatter(d_expand, 'fsdp', scatter_dimension=1, tiled=True)  114 us
    reduce_scatter x2, waiting for transfers between devices, collect_grad(): lax.psum_scatter(term_fn(jnp.int32(0), lax.axis_size('tensor') * row_coun...  88.9 us
    reduce_scatter x1, waiting for transfers between devices, on_device(): lax.psum_scatter(d_down, 'fsdp', scatter_dimension=1, tiled=True)  73.6 us
    reduce_scatter x1, waiting for transfers between devices, on_device(): lax.psum_scatter(d_out, 'fsdp', scatter_dimension=1, tiled=True)  68 us
    all_gather x1, waiting for transfers between devices, on_device(): lax.all_gather(expand_weight[layer_index], 'fsdp', axis=1, tiled=True)  58 us
    squeeze x112, local copies, waits for them, and re-layouts, delta_spans(): lax.scan(jax.checkpoint(advance), (start_mem, start_seg), (blocked(querie...  56.3 us
    reduce_scatter x1, waiting for transfers between devices, on_device(): lax.psum_scatter(d_qkv, 'fsdp', scatter_dimension=1, tiled=True)  54.9 us
  transfers between devices with their start and end apart: 16, of which 14 were waited for; matrix products, arithmetic and copies ran while one was open for 4% of the time, Pallas kernels for 0%

commit v1 on v0

--- a/solution.py
+++ b/solution.py
@@ -342,7 +342,8 @@
     head_parts[layer_index] = d_head_gain
     conv_total = lax.psum(jnp.stack(conv_parts), "fsdp")
     attn_total, ffn_total, head_total = lax.psum(
-        (jnp.stack(attn_parts), jnp.stack(ffn_parts), jnp.stack(head_parts)), ("fsdp", "tensor")
+        lax.psum((jnp.stack(attn_parts), jnp.stack(ffn_parts), jnp.stack(head_parts)), "tensor"),
+        "fsdp",
     )
     qkv_total = jnp.stack([parts[0] for parts in weight_parts])
     beta_total = jnp.stack([parts[1] for parts in weight_parts])

time: 1530 us -> 1530 us (level)
  blocking collectives: 129 us -> 95.7 us
  waiting for transfers between devices: 639 us -> 671 us
    psum x1, blocking collectives: 39.8 us -> 5.98 us  [on_device(): lax.psum((jnp.stack(attn_parts), jnp.stack(ffn_parts), jnp.stack(head_par...]
    reduce_scatter x1, waiting for transfers between devices: 54.9 us -> 76.6 us  [on_device(): lax.psum_scatter(d_qkv, 'fsdp', scatter_dimension=1, tiled=True)]
    unnamed x17, waiting for transfers between devices: 2.64 us -> 18.8 us
  transfers between devices with their start and end apart: 16 -> 16, of which waited for: 14 -> 15; matrix products, arithmetic and copies ran while one was open for 4% -> 4% of each run, Pallas kernels for 0% -> 0%
where the time goes in v1:
time: 1530 us; the launch traced here: 1520 us
  waiting for transfers between devices  671 us (44%)
  other arithmetic  374 us (24%)
  matrix products  263 us (17%)
  blocking collectives  95.7 us (6%)
  local copies, waits for them, and re-layouts  89.4 us (6%)
    another operation x112, other arithmetic, advance(): jax.scipy.linalg.solve_triangular(system, right_side, lower=True, unit_di...  319 us
    reduce_scatter x1, waiting for transfers between devices, on_device(): lax.psum_scatter(d_expand, 'fsdp', scatter_dimension=1, tiled=True)  114 us
    reduce_scatter x2, waiting for transfers between devices, collect_grad(): lax.psum_scatter(term_fn(jnp.int32(0), lax.axis_size('tensor') * row_coun...  88.8 us
    reduce_scatter x1, waiting for transfers between devices, on_device(): lax.psum_scatter(d_qkv, 'fsdp', scatter_dimension=1, tiled=True)  76.6 us
    reduce_scatter x1, waiting for transfers between devices, on_device(): lax.psum_scatter(d_down, 'fsdp', scatter_dimension=1, tiled=True)  73.5 us
    reduce_scatter x1, waiting for transfers between devices, on_device(): lax.psum_scatter(d_out, 'fsdp', scatter_dimension=1, tiled=True)  67.9 us
    all_gather x1, waiting for transfers between devices, on_device(): lax.all_gather(expand_weight[layer_index], 'fsdp', axis=1, tiled=True)  58 us
    squeeze x112, local copies, waits for them, and re-layouts, delta_spans(): lax.scan(jax.checkpoint(advance), (start_mem, start_seg), (blocked(querie...  56.3 us
  transfers between devices with their start and end apart: 16, of which 15 were waited for; matrix products, arithmetic and copies ran while one was open for 4% of the time, Pallas kernels for 0%

profile of v1, /device:TPU:0, one launch (start us, length us, event | category | flops | bytes accessed | tf_op | source)
XLA Modules:
  0.0 1515.1 jit_solution(1637898877853449194)
XLA Ops:
  12.7 22.1 %all-gather = bf16[1,1024,2]{1,2,0:T(2,128)(2,1)S(1)} all-gather(bf16[1,128,2]{1,2,0:T(2,128)(2,1)S(1)} %copy-done.35), channel_id=2, replica_groups=mesh['fsdp'=8,'tensor'=4] {'fsdp'}, dimensions={1}, use_global_device_ids=true | all-gather | bytes 4608 | tf_op jit(solution)/shard_map/all_gather | solution.py:182
  35.0 29.6 %all-gather.2 = bf16[1,256,1024]{2,1,0:T(8,128)(2,1)S(1)} all-gather(bf16[1,256,128]{2,1,0:T(8,128)(2,1)S(1)} %copy-done.29), channel_id=4, replica_groups=mesh['fsdp'=8,'tensor'=4] {'fsdp'}, dimensions={2}, use_global_device_ids=true | all-gather | bytes 589824 | tf_op jit(solution)/shard_map/all_gather | solution.py:184
  64.7 22.7 %all-gather.13.cloned.1.call-done = bf16[1024,1024]{1,0:T(8,128)(2,1)} async-done(((bf16[256,1024]{1,0:T(8,128)(2,1)}), bf16[1024,1024]{1,0:T(8,128)(2,1)}) %all-gather.13.cloned.1.call-update) | async-done | bytes 2097168 | tf_op jit(solution)/shard_map/all_gather | solution.py:136
  104.5 255.6 %while.43 = (s32[]{:T(128)}, f32[2,128,128]{2,1,0:T(8,128)S(1)}, s32[2]{0:T(128)S(1)}, f32[16,2,64,128]{3,2,0,1:T(8,128)S(1)}, f32[16,2,128,128]{3,2,1,0:T(8,128...) while((s32[]{:T(128)}, f32[2,128,128]{2,1,0:T(8,128)S(1)}, ...), condition=%wide.region_4.6_spmd.clone, body=%wide.region_3.5_spmd.clone.sunk | while | flops 126235200 | bytes 2117866 | solution.py:88
  105.0 9.8 custom-call.26
  120.9 9.8 custom-call.26
  136.9 9.8 custom-call.26
  152.9 9.8 custom-call.26
  168.9 9.8 custom-call.26
  184.8 9.8 custom-call.26
  200.8 9.8 custom-call.26
  216.8 9.8 custom-call.26
  232.8 9.8 custom-call.26
  248.7 9.8 custom-call.26
  264.7 9.8 custom-call.26
  280.7 9.8 custom-call.26
  296.7 9.8 custom-call.26
  312.6 9.8 custom-call.26
  328.6 9.8 custom-call.26
  344.6 9.8 custom-call.26
  366.5 44.0 %reduce-scatter.12.cloned.1.call-done = f32[256,1024]{1,0:T(8,128)} async-done(((f32[1024,1024]{1,0:T(8,128)}), f32[256,1024]{1,0:T(8,128)}) %reduce-scatter.12.cloned.1.call-update) | async-done | bytes 1048592 | tf_op jit(solution)/shard_map/reduce_scatter | solution.py:140
  414.6 58.0 %all-gather.23.cloned.1.call-done = bf16[1,2,1024,704]{2,3,1,0:T(8,128)(2,1)} async-done(((bf16[1,2,128,704]{2,3,1,0:T(8,128)(2,1)}), bf16[1,2,1024,704]{2,3,1,0:T(8,128)(2,1)}) %all-gather.23.cloned.1.call-update) | async-done | bytes 2883600 | tf_op jit(solution)/shard_map/all_gather | solution.py:183
  472.6 22.9 %all-gather.15.cloned.1.call-done = bf16[1024,1024]{1,0:T(8,128)(2,1)} async-done(((bf16[256,1024]{1,0:T(8,128)(2,1)}), bf16[1024,1024]{1,0:T(8,128)(2,1)}) %all-gather.15.cloned.1.call-update) | async-done | bytes 2097168 | tf_op jit(solution)/shard_map/all_gather | solution.py:136
  503.6 37.9 %all-gather.25.cloned.1.call-done = bf16[1,704,1024]{2,1,0:T(8,128)(2,1)} async-done(((bf16[1,704,128]{2,1,0:T(8,128)(2,1)}), bf16[1,704,1024]{2,1,0:T(8,128)(2,1)}) %all-gather.25.cloned.1.call-update) | async-done | bytes 1441808 | tf_op jit(solution)/shard_map/all_gather | solution.py:185
  541.5 22.6 %all-gather.17.cloned.1.call-done = bf16[1024,1024]{1,0:T(8,128)(2,1)} async-done(((bf16[256,1024]{1,0:T(8,128)(2,1)}), bf16[1024,1024]{1,0:T(8,128)(2,1)}) %all-gather.17.cloned.1.call-update) | async-done | bytes 2097168 | tf_op jit(solution)/shard_map/all_gather | solution.py:149
  578.5 44.6 %reduce-scatter.16.cloned.1.call-done = f32[256,1024]{1,0:T(8,128)} async-done(((f32[1024,1024]{1,0:T(8,128)}), f32[256,1024]{1,0:T(8,128)}) %reduce-scatter.16.cloned.1.call-update) | async-done | bytes 1048592 | tf_op jit(solution)/shard_map/reduce_scatter | solution.py:153
  626.4 22.2 %all-gather.19.cloned.1.call-done = bf16[1024,1024]{1,0:T(8,128)(2,1)} async-done(((bf16[256,1024]{1,0:T(8,128)(2,1)}), bf16[1024,1024]{1,0:T(8,128)(2,1)}) %all-gather.19.cloned.1.call-update) | async-done | bytes 2097168 | tf_op jit(solution)/shard_map/all_gather | solution.py:149
  658.6 350.7 %while.44 = (s32[]{:T(128)}, f32[2,128,128]{2,1,0:T(8,128)S(1)}, f32[16,2,64,128]{3,2,0,1:T(8,128)}, f32[16,2,64,128]{3,2,0,1:T(8,128)}, f32[16,2,64,128]{3,2,0,...) while((s32[]{:T(128)}, f32[2,128,128]{2,1,0:T(8,128)S(1)}, ...), condition=%wide.region_15.17_spmd.clone, body=%wide.region_12.16_spmd.clone.sunk | while | flops 321565120 | bytes 5879079 | solution.py:88
  663.3 9.8 custom-call.27
  685.2 9.8 custom-call.27
  707.1 9.8 custom-call.27
  729.0 9.8 custom-call.27
  751.0 9.8 custom-call.27
  772.9 9.8 custom-call.27
  794.8 9.8 custom-call.27
  816.7 9.8 custom-call.27
  838.6 9.8 custom-call.27
  860.6 9.8 custom-call.27
  882.5 9.8 custom-call.27
  904.4 9.8 custom-call.27
  948.2 9.8 custom-call.27
  1062.2 16.2 %reduce-scatter.28.cloned.1.call-done = f32[128,2]{1,0:T(8,128)} async-done(((f32[1024,2]{1,0:T(8,128)}), f32[128,2]{1,0:T(8,128)}) %reduce-scatter.28.cloned.1.call-update) | async-done | bytes 1040
  1079.9 76.6 %reduce-scatter.20.cloned.1.call-done = f32[3,128,256]{1,2,0:T(8,128)} async-done(((f32[3,1024,256]{1,2,0:T(8,128)}), f32[3,128,256]{1,2,0:T(8,128)}) %reduce-scatter.20.cloned.1.call-update) | async-done | bytes 393232 | tf_op jit(solution)/shard_map/reduce_scatter | solution.py:333
  1158.4 44.2 %reduce-scatter.18.cloned.1.call-done = f32[256,1024]{1,0:T(8,128)} async-done(((f32[1024,1024]{1,0:T(8,128)}), f32[256,1024]{1,0:T(8,128)}) %reduce-scatter.18.cloned.1.call-update) | async-done | bytes 1048592 | tf_op jit(solution)/shard_map/reduce_scatter | solution.py:153
  1210.3 38.0 %all-reduce.31 = (f32[1,1024]{1,0:T(1,128)}, f32[1,1024]{1,0:T(1,128)}, f32[1,128]{1,0:T(1,128)}, f32[1,3,4,256]{3,2,1,0:T(4,128)}) all-reduce(f32[1,1024]{1,0:T(1,128)S(1)} %get-tuple-element.738, f32[1,1024]{1,0:T(1,128)S(1)} %get-tuple-element.739, ...), channel_id=1, replica_groups=mesh['fsdp'=8,'tensor'=4] {'fsdp'}, use_global_device_ids=true, to_apply=%region_22.24 | all-reduce | flops 5248 | bytes 41984 | tf_op jit(solution)/shard_map/psum | solution.py:344
  1252.9 73.5 %reduce-scatter.26.cloned.1.call-done = f32[704,128]{1,0:T(8,128)} async-done(((f32[704,1024]{1,0:T(8,128)}), f32[704,128]{1,0:T(8,128)}) %reduce-scatter.26.cloned.1.call-update) | async-done | bytes 360464 | tf_op jit(solution)/shard_map/reduce_scatter | solution.py:337
  1326.4 114.1 %reduce-scatter.24.cloned.1.call-done = f32[2,128,704]{1,2,0:T(8,128)} async-done(((f32[2,1024,704]{1,2,0:T(8,128)}), f32[2,128,704]{1,2,0:T(8,128)}) %reduce-scatter.24.cloned.1.call-update) | async-done | bytes 720912 | tf_op jit(solution)/shard_map/reduce_scatter | solution.py:335
  1440.5 67.9 %reduce-scatter.22.cloned.1.call-done = f32[256,128]{1,0:T(8,128)} async-done(((f32[256,1024]{1,0:T(8,128)}), f32[256,128]{1,0:T(8,128)}) %reduce-scatter.22.cloned.1.call-update) | async-done | bytes 131088 | tf_op jit(solution)/shard_map/reduce_scatter | solution.py:336
  (1097 shorter events, 453.3 us)
Async XLA Ops:
  7.2 4.2 copy-start.34
  7.2 4.7 copy-start.31
  7.2 5.5 copy-start.35
  7.2 27.8 %copy-start.32 = (f32[1,3,4,256]{3,2,1,0:T(4,128)S(1)}, f32[1,3,4,256]{3,2,1,0:T(4,128)}, u32[]{:S(2)}) copy-start(f32[1,3,4,256]{3,2,1,0:T(4,128)} %param.27) | copy-start | bytes 36868
  7.2 27.8 %copy-start.29 = (bf16[1,256,128]{2,1,0:T(8,128)(2,1)S(1)}, bf16[1,256,128]{2,1,0:T(8,128)(2,1)}, u32[]{:S(2)}) copy-start(bf16[1,256,128]{2,1,0:T(8,128)(2,1)} %param.28) | copy-start | bytes 196612
  7.2 57.4 %all-gather.21.cloned.1.call-start = ((), (), s32[]{:S(2)}) async-start(), calls=%async_computation.21 | async-start | bytes 1769472 | tf_op jit(solution)/shard_map/all_gather | solution.py:181
  8.0 79.4 %all-gather.13.cloned.1.call-start = ((), (), s32[]{:S(2)}) async-start(), calls=%async_computation.9 | async-start | bytes 2621440 | tf_op jit(solution)/shard_map/all_gather | solution.py:136
  11.3 399.2 %reduce-scatter.12.cloned.1.call-start = ((), (), s32[]{:S(2)}) async-start(), calls=%async_computation.10 | async-start | bytes 5242880 | tf_op jit(solution)/shard_map/reduce_scatter | solution.py:140
  64.7 298.3 %copy-start.21 = (bf16[1,256,1024]{2,1,0:T(8,128)(2,1)}, bf16[1,256,1024]{2,1,0:T(8,128)(2,1)S(1)}, u32[]{:S(2)}) copy-start(bf16[1,256,1024]{2,1,0:T(8,128)(2,1)S(1)} %all-gather.2) | copy-start | bytes 1572868
  91.2 1.7 copy-start.7
  92.9 2.9 copy-start.11
  92.9 2.9 copy-start.13
  92.9 4.8 copy-start.9
  101.6 2.0 copy-start.17
  104.5 256.1 %copy-start.33 = (f32[1,128]{1,0:T(1,128)S(1)}, f32[1,128]{1,0:T(1,128)}, u32[]{:S(2)}) copy-start(f32[1,128]{1,0:T(1,128)} %param.24) | copy-start | bytes 1540
  360.1 5.7 copy-start.20
  363.0 2.8 copy-start.19
  365.8 44.7 %copy-start.5 = (bf16[256,1024]{1,0:T(8,128)(2,1)S(1)}, bf16[256,1024]{1,0:T(8,128)(2,1)}, u32[]{:S(2)}) copy-start(bf16[256,1024]{1,0:T(8,128)(2,1)} %param.19) | copy-start | bytes 1572868
  365.8 46.1 %copy-start.28 = (f32[1,1024]{1,0:T(1,128)S(1)}, f32[1,1024]{1,0:T(1,128)}, u32[]{:S(2)}) copy-start(f32[1,1024]{1,0:T(1,128)} %param.23) | copy-start | bytes 12292
  365.8 106.8 %all-gather.23.cloned.1.call-start = ((), (), s32[]{:S(2)}) async-start(), calls=%async_computation.22 | async-start | bytes 3244032 | tf_op jit(solution)/shard_map/all_gather | solution.py:183
  366.4 129.1 %all-gather.15.cloned.1.call-start = ((), (), s32[]{:S(2)}) async-start(), calls=%async_computation.11 | async-start | bytes 2621440 | tf_op jit(solution)/shard_map/all_gather | solution.py:136
  412.9 128.5 %all-gather.25.cloned.1.call-start = ((), (), s32[]{:S(2)}) async-start(), calls=%async_computation.23 | async-start | bytes 1622016 | tf_op jit(solution)/shard_map/all_gather | solution.py:185
  413.5 150.6 %all-gather.17.cloned.1.call-start = ((), (), s32[]{:S(2)}) async-start(), calls=%async_computation.13 | async-start | bytes 2621440 | tf_op jit(solution)/shard_map/all_gather | solution.py:149
  414.2 208.8 %reduce-scatter.16.cloned.1.call-start = ((), (), s32[]{:S(2)}) async-start(), calls=%async_computation.14 | async-start | bytes 5242880 | tf_op jit(solution)/shard_map/reduce_scatter | solution.py:153
  564.1 9.3 copy-start.36
  578.4 46.2 %copy-start.23 = (bf16[256,1024]{1,0:T(8,128)(2,1)S(1)}, bf16[256,1024]{1,0:T(8,128)(2,1)}, u32[]{:S(2)}) copy-start(bf16[256,1024]{1,0:T(8,128)(2,1)} %param.31) | copy-start | bytes 1572868
  578.4 70.1 %all-gather.19.cloned.1.call-start = ((), (), s32[]{:S(2)}) async-start(), calls=%async_computation.15 | async-start | bytes 2621440 | tf_op jit(solution)/shard_map/all_gather | solution.py:149
  623.0 1.6 copy-start.15
  624.6 23.9 %copy-start.22 = (bf16[1,256,1024]{2,1,0:T(8,128)(2,1)S(1)}, bf16[1,256,1024]{2,1,0:T(8,128)(2,1)}, u32[]{:S(2)}) copy-start(bf16[1,256,1024]{2,1,0:T(8,128)(2,1)} %copy-done.21) | copy-start | bytes 1572868
  625.8 452.6 %reduce-scatter.28.cloned.1.call-start = ((), (), s32[]{:S(2)}) async-start(), calls=%async_computation.24 | async-start | bytes 589824
  653.4 1.9 copy-start
  1009.3 2.1 copy-start.3
  1016.4 140.1 %reduce-scatter.20.cloned.1.call-start = ((), (), s32[]{:S(2)}) async-start(), calls=%async_computation.17 | async-start | bytes 3538944 | tf_op jit(solution)/shard_map/reduce_scatter | solution.py:333
  1016.6 4.2 copy-start.8
  1016.6 4.2 copy-start.10
  1016.7 4.2 copy-start.12
  1016.7 4.2 copy-start.14
  1027.8 1.8 copy-start.18
  1033.1 169.5 %reduce-scatter.18.cloned.1.call-start = ((), (), s32[]{:S(2)}) async-start(), calls=%async_computation.16 | async-start | bytes 5242880 | tf_op jit(solution)/shard_map/reduce_scatter | solution.py:153
  1038.7 211.0 %reduce-scatter.14.cloned.1.call-start = ((), (), s32[]{:S(2)}) async-start(), calls=%async_computation.12 | async-start | bytes 5242880 | tf_op jit(solution)/shard_map/reduce_scatter | solution.py:140
  1044.4 282.0 %reduce-scatter.26.cloned.1.call-start = ((), (), s32[]{:S(2)}) async-start(), calls=%async_computation.20 | async-start | bytes 3244032 | tf_op jit(solution)/shard_map/reduce_scatter | solution.py:337
  1049.7 390.8 %reduce-scatter.24.cloned.1.call-start = ((), (), s32[]{:S(2)}) async-start(), calls=%async_computation.19 | async-start | bytes 6488064 | tf_op jit(solution)/shard_map/reduce_scatter | solution.py:335
  1058.1 3.8 copy-start.1
  1058.1 450.3 %reduce-scatter.22.cloned.1.call-start = ((), (), s32[]{:S(2)}) async-start(), calls=%async_computation.18 | async-start | bytes 1179648 | tf_op jit(solution)/shard_map/reduce_scatter | solution.py:336
  1061.8 140.9 %copy-start.30 = (f32[1,1024]{1,0:T(1,128)S(1)}, f32[1,1024]{1,0:T(1,128)}, u32[]{:S(2)}) copy-start(f32[1,1024]{1,0:T(1,128)} %param.22) | copy-start | bytes 12292
  1062.2 187.5 %copy-start.6 = (bf16[256,1024]{1,0:T(8,128)(2,1)S(1)}, bf16[256,1024]{1,0:T(8,128)(2,1)}, u32[]{:S(2)}) copy-start(bf16[256,1024]{1,0:T(8,128)(2,1)} %param.19) | copy-start | bytes 1572868
  1062.2 187.5 %copy-start.16 = (f32[256,1024]{1,0:T(8,128)S(1)}, f32[256,1024]{1,0:T(8,128)}, u32[]{:S(2)}) copy-start(f32[256,1024]{1,0:T(8,128)} %reduce-scatter.16.cloned.1.call-done) | copy-start | bytes 3145732
  1062.2 187.5 %copy-start.24 = (bf16[256,1024]{1,0:T(8,128)(2,1)S(1)}, bf16[256,1024]{1,0:T(8,128)(2,1)}, u32[]{:S(2)}) copy-start(bf16[256,1024]{1,0:T(8,128)(2,1)} %param.31) | copy-start | bytes 1572868
  (8 other events, 10.1 us)
Sparse Core Ops, SparseCore 0:
  10.2 50.5 all-gather.20
  62.9 24.3 all-gather.12
  365.9 44.4 reduce-scatter.11
  412.6 60.0 all-gather.22
  474.7 20.7 all-gather.14
  497.6 43.8 all-gather.24
  543.1 20.9 all-gather.16
  578.5 44.4 reduce-scatter.15
  625.9 22.5 all-gather.18
  1016.5 61.8 reduce-scatter.27
  1082.4 73.9 reduce-scatter.19
  1159.0 43.5 reduce-scatter.17
  1205.1 44.4 reduce-scatter.13
  1254.1 72.2 reduce-scatter.25
  1330.9 109.5 reduce-scatter.23
  1444.7 63.5 reduce-scatter.21
